TPU v7x, 32 devices: a whole 2x2x4 slice. The times are simulated.
32 devices in a mesh: gx: 8 (over y, x, core), gy: 4 (over z).
Axes of the slice: x: 2, y: 2, z: 4, core: 2. Of those that a mesh axis runs over, the one named last changes fastest.
Arguments:
- points_rhs: float32 [16, 524288], P(None, ('gx', 'gy')), may hold values from -6 to 6
- morton_order: int32 [524288], P(('gx', 'gy')), may hold values from 0 to 16383, as said below
- band_offsets: int32 [2048], P(('gx', 'gy')), may hold values from -16 to 16, as said below
- leaf_basis: bfloat16 [2048, 32, 256], P(('gx', 'gy')), may hold values from -0.375 to 0.375
- band_blocks: bfloat16 [2048, 2, 256, 256], P(('gx', 'gy')), may hold values from -0.375 to 0.375
- translations: float32 [32, 5, 8, 2, 32, 32], P(('gx', 'gy'))
- out_basis: bfloat16 [2048, 32, 256], P(('gx', 'gy')), may hold values from -1 to 1
Outputs:
- transformed: float32 [16, 524288], P(None, ('gx', 'gy'))
Inputs may be any that keep to these rules, and one draw needn't show every extreme that they name: `morton_order`: for every node k, entries 16384 * k to 16384 * (k + 1) - 1 hold each of 0 to 16383 exactly once. `band_offsets`: never zero; the first leaf of every node has offset -16 and the last leaf of every node has offset 16.
All inputs are finite; a program needn't handle non-finite values.
Results may differ from a plain program's by a relative error of at most 0.0033.
Values may be sent and summed in bfloat16 or wider, within the bound.
A program may use at most 128 MiB of HBM per device.

v0:
```python
import jax
import jax.numpy as jnp
from jax import lax
from jax.sharding import PartitionSpec as P

HW = 16


def from_partner(x, axis, distance):
    return lax.ppermute(x, axis, [(i, i ^ 1 << distance) for i in range(lax.axis_size(axis))])


def extended(x, sides, width):
    for axis, dim in sides:
        count, length = (lax.axis_size(axis), x.shape[dim])
        up = [(i, (i + 1) % count) for i in range(count - 1)]
        down = [(j, i) for i, j in up]
        last = lax.slice_in_dim(x, length - width, length, axis=dim)
        initial = lax.slice_in_dim(x, 0, width, axis=dim)
        before = lax.ppermute(last, axis, up)
        after = lax.ppermute(initial, axis, down)
        x = jnp.concatenate([before, x, after], axis=dim)
    return x


def translate(level_weights, own_coeffs, other_coeffs):
    first = jnp.einsum(
        "gab,bgm->agm",
        level_weights[:, 0],
        own_coeffs,
        precision=lax.Precision.HIGHEST,
        preferred_element_type=jnp.float32,
    )
    second = jnp.einsum(
        "gab,bgm->agm",
        level_weights[:, 1],
        other_coeffs,
        precision=lax.Precision.HIGHEST,
        preferred_element_type=jnp.float32,
    )
    return first + second


def local(points_rhs, morton_order, band_offsets, leaf_basis, band_blocks, translations, out_basis):
    rhs_count, point_count = points_rhs.shape
    leaf_count, rank_size, leaf_size = leaf_basis.shape
    group_total = translations.shape[2]
    total_cols = leaf_count * rhs_count
    group_width = total_cols // group_total
    ordered = points_rhs[:, morton_order].astype(jnp.bfloat16)
    leaves = ordered.reshape(rhs_count, leaf_count, leaf_size)
    coeffs = jnp.einsum(
        "lrp,slp->rls", leaf_basis, leaves, preferred_element_type=jnp.float32
    ).reshape(rank_size, total_cols)
    weights = translations[0]
    low_bits = lax.axis_size("gy").bit_length() - 1
    high_bits = lax.axis_size("gx").bit_length() - 1
    coeffs = coeffs.reshape(rank_size, group_total, group_width)
    for level_bit in range(low_bits):
        partner = from_partner(coeffs, "gy", level_bit)
        coeffs = translate(weights[level_bit], coeffs, partner)
    for level_bit in range(high_bits):
        partner = from_partner(coeffs, "gx", level_bit)
        coeffs = translate(weights[low_bits + level_bit], coeffs, partner)
    coeffs = coeffs.reshape(rank_size, total_cols)
    coeff_bf = coeffs.astype(jnp.bfloat16).reshape(rank_size, leaf_count, rhs_count)
    far_term = jnp.einsum("lrp,rls->slp", out_basis, coeff_bf, preferred_element_type=jnp.float32)
    padded = extended(ordered, ((("gx", "gy"), 1),), HW * leaf_size)
    blocks_all = padded.reshape(rhs_count, leaf_count + 2 * HW, leaf_size)
    block_index = jnp.arange(leaf_count, dtype=jnp.int32) + HW + band_offsets
    picked = jnp.take(blocks_all, block_index, axis=1)
    own_term = jnp.einsum(
        "lpq,slq->slp", band_blocks[:, 0], leaves, preferred_element_type=jnp.float32
    )
    partner_term = jnp.einsum(
        "lpq,slq->slp", band_blocks[:, 1], picked, preferred_element_type=jnp.float32
    )
    return (far_term + own_term + partner_term).reshape(rhs_count, point_count)


def solution(mesh):
    return jax.shard_map(
        local,
        mesh=mesh,
        in_specs=(
            P(None, ("gx", "gy")),
            P(("gx", "gy")),
            P(("gx", "gy")),
            P(("gx", "gy"), None, None),
            P(("gx", "gy"), None, None, None),
            P(("gx", "gy"), None, None, None, None, None),
            P(("gx", "gy"), None, None),
        ),
        out_specs=P(None, ("gx", "gy")),
        check_vma=False,
    )
```

profile of v0, /device:TPU:0, one launch (start us, length us, event | category | flops | bytes accessed | tf_op | source)
XLA Modules:
  0.0 126.0 jit_solution(5928063699301836887)
XLA Ops:
  0.0 0.0 copy-start
  0.0 0.0 copy-start.8
  0.0 4.7 %copy.52 = bf16[16,16384]{0,1:T(8,128)(2,1)} copy(f32[16,16384]{1,0:T(8,128)} %param.7) | data formatting | bytes 1572864 | tf_op args[0]
  4.7 0.0 copy-done.8
  4.7 57.7 %gather_fusion = bf16[16384,16]{1,0:T(8,128)(2,1)} fusion(bf16[16,16384]{0,1:T(8,128)(2,1)} %copy.52, s32[16384]{0:T(1024)S(1)} %fusion.23), kind=kCustom, calls=%fused_computation | custom fusion | bytes 1114112 | tf_op jit(solution)/shard_map/gather | solution.py:50
  62.4 1.7 %fusion.25 = (bf16[16,4096]{0,1:T(8,128)(2,1)S(1)}, bf16[16,4096]{0,1:T(8,128)(2,1)S(1)}) fusion(bf16[16,16384]{0,1:T(8,128)(2,1)} %bitcast.98), kind=kLoop, calls=%fused_computation.54 | loop fusion | bytes 524288 | tf_op jit(solution)/shard_map/slice | solution.py:18
  64.1 1.0 copy.65
  65.1 1.3 %collective-permute-start.6 = (bf16[16,4096]{1,0:T(8,128)(2,1)}, bf16[16,4096]{1,0:T(8,128)(2,1)S(1)}, u32[]{:S(2)}, u32[]{:S(2)}) collective-permute-start(bf16[16,4096]{1,0:T(8,128)(2,1)} %copy.65), channel_id=1, source_target_pairs={{1,0},{2,1},{3,2},{4,3},{5,4},{6,5},{7,6},{8,7},{9,8},{10,9},{11,1... | collective-permute-start | bytes 393224 | tf_op jit(solution)/shard_map/ppermute | solution.py:21
  66.4 1.0 copy.64
  67.3 6.2 %collective-permute-start.5 = (bf16[16,4096]{1,0:T(8,128)(2,1)}, bf16[16,4096]{1,0:T(8,128)(2,1)}, u32[]{:S(2)}, u32[]{:S(2)}) collective-permute-start(bf16[16,4096]{1,0:T(8,128)(2,1)} %copy.64), channel_id=1, source_target_pairs={{0,1},{1,2},{2,3},{3,4},{4,5},{5,6},{6,7},{7,8},{8,9},{9,10},{10,1... | collective-permute-start | bytes 393224 | tf_op jit(solution)/shard_map/ppermute | solution.py:20
  73.6 3.7 %fusion.27 = f32[64,16,32]{2,1,0:T(8,128)S(1)} fusion(bf16[16,64,256]{0,2,1:T(8,128)(2,1)} %bitcast.99, bf16[64,32,256]{2,1,0:T(8,128)(2,1)} %param.10), kind=kOutput, calls=%fused_computation.56 | convolution fusion | flops 16777216 | bytes 1703936 | tf_op jit(solution)/shard_map/lrp,slp->rls/dot_general | solution.py:52
  77.3 0.8 copy.56
  78.1 0.0 copy-start.1
  78.1 0.0 copy-start.9
  78.1 1.4 %collective-permute-start = (f32[32,8,128]{2,0,1:T(8,128)}, f32[32,8,128]{2,0,1:T(8,128)}, u32[]{:S(2)}, u32[]{:S(2)}) collective-permute-start(f32[32,8,128]{2,0,1:T(8,128)} %copy.56), channel_id=1, source_target_pairs={{0,1},{1,0},{2,3},{3,2},{4,5},{5,4},{6,7},{7,6},{8,9},{9,8},{10,11... | collective-permute-start | bytes 393224 | tf_op jit(solution)/shard_map/ppermute | solution.py:10
  79.5 6.9 %fusion.2 = f32[64,16,256]{2,1,0:T(8,128)S(1)} fusion(bf16[16,64,256]{0,2,1:T(8,128)(2,1)} %bitcast.100, bf16[64,2,256,256]{3,2,1,0:T(8,128)(2,1)} %param.11), kind=kOutput, calls=%fused_computation.4 | convolution fusion | flops 134217728 | bytes 13631488 | tf_op jit(solution)/shard_map/lpq,slq->slp/dot_general | solution.py:72
  86.4 0.0 copy-done.1
  86.4 0.9 fusion.26
  87.3 0.0 copy-start.5
  87.3 1.6 %fusion.22 = f32[8,128,32]{1,2,0:T(8,128)} fusion(f32[32,8,128]{0,2,1:T(8,128)S(1)} %bitcast.103, f32[8,2,32,32]{3,2,0,1:T(8,128)S(1)} %bitcast.115), kind=kOutput, calls=%fused_computation.48 | convolution fusion | flops 12582912 | bytes 786432 | tf_op jit(solution)/shard_map/gab,bgm->agm/dot_general | solution.py:27
  88.9 0.0 copy-done.5
  88.9 0.0 copy-done.9
  88.9 3.5 %copy.66 = bf16[16,16384]{1,0:T(8,128)(2,1)S(1)} copy(bf16[16,16384]{0,1:T(8,128)(2,1)} %bitcast.101) | data formatting | bytes 1048576 | tf_op jit(solution)/shard_map/convert_element_type | solution.py:50
  92.3 0.0 copy-start.6
  92.4 0.0 copy-start.7
  92.4 1.7 %copy.92 = f32[1,1,8,2,32,32]{5,4,2,3,1,0:T(8,128)} copy(f32[1,1,8,2,32,32]{5,4,3,2,1,0:T(8,128)} %get-tuple-element.12) | data formatting | bytes 131072
  94.1 0.7 copy.91
  94.8 0.7 copy.90
  95.5 0.0 collective-permute-done.6
  95.5 0.0 collective-permute-done.5
  95.6 1.0 pad_maximum_fusion
  96.5 0.1 copy.88
  96.6 0.0 collective-permute-done
  96.6 0.0 copy-done.6
  96.6 0.0 copy-done.7
  96.6 1.2 fusion.11
  97.8 4.2 %collective-permute-start.1 = (f32[32,8,128]{2,0,1:T(8,128)S(1)}, f32[32,8,128]{2,0,1:T(8,128)}, u32[]{:S(2)}, u32[]{:S(2)}) collective-permute-start(f32[32,8,128]{2,0,1:T(8,128)S(1)} %fusion.11), channel_id=1, source_target_pairs={{0,2},{1,3},{2,0},{3,1},{4,6},{5,7},{6,4},{7,5},{8,10},{9,11},{10,... | collective-permute-start | bytes 393224 | tf_op jit(solution)/shard_map/ppermute | solution.py:10
  101.9 1.4 %gather_fusion.1 = bf16[64,16,256]{2,1,0:T(8,128)(2,1)} fusion(bf16[16,96,256]{2,0,1:T(8,128)(2,1)S(1)} %bitcast.105, s32[1024]{0:T(1024)S(1)} %pad_clamp_fusion), kind=kCustom, calls=%fused_computation.1 | custom fusion | bytes 1048832 | tf_op jit(solution)/shard_map/jit(_take)/gather | solution.py:71
  103.3 0.0 copy-start.4
  103.3 0.0 copy-start.3
  103.3 0.0 copy-start.2
  103.3 5.9 %fusion = f32[64,16,256]{2,1,0:T(8,128)S(1)} fusion(bf16[64,2,256,256]{3,2,1,0:T(8,128)(2,1)} %param.11, bf16[64,16,256]{2,1,0:T(8,128)(2,1)} %gather_fusion.1, pred[64]{0:T(512)(128)(4,1)S(1)} %get-tuple-element.5), kind=kOutput, calls=%fused_computation.2 | convolution fusion | flops 134479872 | bytes 9961536 | tf_op jit(solution)/shard_map/lpq,slq->slp/dot_general | solution.py:75
  109.2 0.0 copy-done.4
  109.2 0.3 fusion.21
  109.5 0.0 collective-permute-done.1
  109.5 1.2 fusion.10
  110.7 0.2 collective-permute-start.2
  110.9 0.0 copy-done.3
  110.9 0.3 fusion.20
  111.2 0.9 collective-permute-done.2
  112.1 0.3 fusion.9
  112.4 2.3 %collective-permute-start.3 = (f32[32,8,128]{2,0,1:T(8,128)S(1)}, f32[32,8,128]{2,0,1:T(8,128)S(1)}, u32[]{:S(2)}, u32[]{:S(2)}) collective-permute-start(f32[32,8,128]{2,0,1:T(8,128)S(1)} %fusion.9), channel_id=1, source_target_pairs={{0,8},{4,12},{8,0},{12,4},{16,24},{20,28},{24,16},{28,20},{1,9},{5... | collective-permute-start | bytes 393224 | tf_op jit(solution)/shard_map/ppermute | solution.py:10
  114.7 0.0 copy-done.2
  114.7 0.3 fusion.19
  114.9 3.7 %collective-permute-done.3 = f32[32,8,128]{2,0,1:T(8,128)S(1)} collective-permute-done((f32[32,8,128]{2,0,1:T(8,128)S(1)}, f32[32,8,128]{2,0,1:T(8,128)S(1)}, u32[]{:S(2)}, u32[]{:S(2)}) %collective-permute-start.3) | collective-permute-done | bytes 131104 | tf_op jit(solution)/shard_map/ppermute | solution.py:10
  118.7 0.3 fusion.8
  118.9 0.9 collective-permute-start.4
  119.9 0.3 fusion.18
  120.1 4.1 %collective-permute-done.4 = f32[32,8,128]{2,0,1:T(8,128)S(1)} collective-permute-done((f32[32,8,128]{2,0,1:T(8,128)S(1)}, f32[32,8,128]{2,0,1:T(8,128)S(1)}, u32[]{:S(2)}, u32[]{:S(2)}) %collective-permute-start.4) | collective-permute-done | bytes 131104 | tf_op jit(solution)/shard_map/ppermute | solution.py:10
  124.2 0.3 fusion.13
  124.4 0.2 copy.61
  124.6 0.0 copy-done
  124.6 0.3 fusion.7
  124.9 1.1 copy.81
  (5 shorter events, 0.1 us)
Async XLA Ops:
  0.0 124.6 %copy-start = (bf16[64,32,256]{2,1,0:T(8,128)(2,1)S(1)}, bf16[64,32,256]{2,1,0:T(8,128)(2,1)}, u32[]{:S(2)}) copy-start(bf16[64,32,256]{2,1,0:T(8,128)(2,1)} %param.13) | copy-start | bytes 3145732
  0.0 4.7 %copy-start.8 = (s32[16384]{0:T(1024)S(1)}, s32[16384]{0:T(1024)}, u32[]{:S(2)}) copy-start(s32[16384]{0:T(1024)} %param.8) | copy-start | bytes 196612
  65.1 30.5 %collective-permute-start.6 = (bf16[16,4096]{1,0:T(8,128)(2,1)}, bf16[16,4096]{1,0:T(8,128)(2,1)S(1)}, u32[]{:S(2)}, u32[]{:S(2)}) collective-permute-start(bf16[16,4096]{1,0:T(8,128)(2,1)} %copy.65), channel_id=1, source_target_pairs={{1,0},{2,1},{3,2},{4,3},{5,4},{6,5},{7,6},{8,7},{9,8},{10,9},{11,1... | collective-permute-start | bytes 393224 | tf_op jit(solution)/shard_map/ppermute | solution.py:21
  67.3 28.2 %collective-permute-start.5 = (bf16[16,4096]{1,0:T(8,128)(2,1)}, bf16[16,4096]{1,0:T(8,128)(2,1)}, u32[]{:S(2)}, u32[]{:S(2)}) collective-permute-start(bf16[16,4096]{1,0:T(8,128)(2,1)} %copy.64), channel_id=1, source_target_pairs={{0,1},{1,2},{2,3},{3,4},{4,5},{5,6},{6,7},{7,8},{8,9},{9,10},{10,1... | collective-permute-start | bytes 393224 | tf_op jit(solution)/shard_map/ppermute | solution.py:20
  78.1 8.3 %copy-start.1 = (f32[1,5,8,2,32,32]{5,4,3,2,1,0:T(8,128)S(1)}, f32[1,5,8,2,32,32]{5,4,3,2,1,0:T(8,128)}, u32[]{:S(2)}) copy-start(f32[1,5,8,2,32,32]{5,4,3,2,1,0:T(8,128)} %param.12) | copy-start | bytes 983044
  78.1 10.8 %copy-start.9 = (s32[64]{0:T(128)S(1)}, s32[64]{0:T(128)}, u32[]{:S(2)}) copy-start(s32[64]{0:T(128)} %param.9) | copy-start | bytes 772
  78.1 18.5 %collective-permute-start = (f32[32,8,128]{2,0,1:T(8,128)}, f32[32,8,128]{2,0,1:T(8,128)}, u32[]{:S(2)}, u32[]{:S(2)}) collective-permute-start(f32[32,8,128]{2,0,1:T(8,128)} %copy.56), channel_id=1, source_target_pairs={{0,1},{1,0},{2,3},{3,2},{4,5},{5,4},{6,7},{7,6},{8,9},{9,8},{10,11... | collective-permute-start | bytes 393224 | tf_op jit(solution)/shard_map/ppermute | solution.py:10
  87.3 1.6 %copy-start.5 = (f32[1,1,8,2,32,32]{5,4,2,3,1,0:T(8,128)}, f32[1,1,8,2,32,32]{5,4,2,3,1,0:T(8,128)S(1)}, u32[]{:S(2)}) copy-start(f32[1,1,8,2,32,32]{5,4,2,3,1,0:T(8,128)S(1)} %copy.93) | copy-start | bytes 196612
  92.3 4.2 %copy-start.6 = (f32[1,1,8,2,32,32]{5,4,2,3,1,0:T(8,128)S(1)}, f32[1,1,8,2,32,32]{5,4,2,3,1,0:T(8,128)}, u32[]{:S(2)}) copy-start(f32[1,1,8,2,32,32]{5,4,2,3,1,0:T(8,128)} %copy-done.5) | copy-start | bytes 196612
  92.4 4.2 %copy-start.7 = (f32[8,128,32]{1,2,0:T(8,128)S(1)}, f32[8,128,32]{1,2,0:T(8,128)}, u32[]{:S(2)}) copy-start(f32[8,128,32]{1,2,0:T(8,128)} %fusion.22) | copy-start | bytes 393220
  97.8 11.8 %collective-permute-start.1 = (f32[32,8,128]{2,0,1:T(8,128)S(1)}, f32[32,8,128]{2,0,1:T(8,128)}, u32[]{:S(2)}, u32[]{:S(2)}) collective-permute-start(f32[32,8,128]{2,0,1:T(8,128)S(1)} %fusion.11), channel_id=1, source_target_pairs={{0,2},{1,3},{2,0},{3,1},{4,6},{5,7},{6,4},{7,5},{8,10},{9,11},{10,... | collective-permute-start | bytes 393224 | tf_op jit(solution)/shard_map/ppermute | solution.py:10
  103.3 5.9 %copy-start.4 = (f32[1,1,8,2,32,32]{5,4,2,3,1,0:T(8,128)S(1)}, f32[1,1,8,2,32,32]{5,4,2,3,1,0:T(8,128)}, u32[]{:S(2)}) copy-start(f32[1,1,8,2,32,32]{5,4,2,3,1,0:T(8,128)} %copy.92) | copy-start | bytes 196612
  103.3 7.6 %copy-start.3 = (f32[1,1,8,2,32,32]{5,4,2,3,1,0:T(8,128)S(1)}, f32[1,1,8,2,32,32]{5,4,2,3,1,0:T(8,128)}, u32[]{:S(2)}) copy-start(f32[1,1,8,2,32,32]{5,4,2,3,1,0:T(8,128)} %copy.91) | copy-start | bytes 196612
  103.3 11.3 %copy-start.2 = (f32[1,1,8,2,32,32]{5,4,2,3,1,0:T(8,128)S(1)}, f32[1,1,8,2,32,32]{5,4,2,3,1,0:T(8,128)}, u32[]{:S(2)}) copy-start(f32[1,1,8,2,32,32]{5,4,2,3,1,0:T(8,128)} %copy.90) | copy-start | bytes 196612
  110.7 1.4 %collective-permute-start.2 = (f32[32,8,128]{2,0,1:T(8,128)S(1)}, f32[32,8,128]{2,0,1:T(8,128)S(1)}, u32[]{:S(2)}, u32[]{:S(2)}) collective-permute-start(f32[32,8,128]{2,0,1:T(8,128)S(1)} %fusion.10), channel_id=1, source_target_pairs={{0,4},{4,0},{8,12},{12,8},{16,20},{20,16},{24,28},{28,24},{1,5},{5... | collective-permute-start | bytes 393224 | tf_op jit(solution)/shard_map/ppermute | solution.py:10
  112.4 6.3 %collective-permute-start.3 = (f32[32,8,128]{2,0,1:T(8,128)S(1)}, f32[32,8,128]{2,0,1:T(8,128)S(1)}, u32[]{:S(2)}, u32[]{:S(2)}) collective-permute-start(f32[32,8,128]{2,0,1:T(8,128)S(1)} %fusion.9), channel_id=1, source_target_pairs={{0,8},{4,12},{8,0},{12,4},{16,24},{20,28},{24,16},{28,20},{1,9},{5... | collective-permute-start | bytes 393224 | tf_op jit(solution)/shard_map/ppermute | solution.py:10
  118.9 5.3 %collective-permute-start.4 = (f32[32,8,128]{2,0,1:T(8,128)S(1)}, f32[32,8,128]{2,0,1:T(8,128)S(1)}, u32[]{:S(2)}, u32[]{:S(2)}) collective-permute-start(f32[32,8,128]{2,0,1:T(8,128)S(1)} %fusion.8), channel_id=1, source_target_pairs={{0,16},{4,20},{8,24},{12,28},{16,0},{20,4},{24,8},{28,12},{1,17},{... | collective-permute-start | bytes 393224 | tf_op jit(solution)/shard_map/ppermute | solution.py:10
where the time goes:
time: 126 us
  local copies, waits for them, and re-layouts  77 us (61%)
  matrix products  22.5 us (18%)
  starting transfers between devices  16.5 us (13%)
  waiting for transfers between devices  8.73 us (7%)
    gather x1, local copies, waits for them, and re-layouts, local(): ordered = points_rhs[:, morton_order].astype(jnp.bfloat16)  57.7 us
    ppermute x5, starting transfers between devices, from_partner(): lax.ppermute(x, axis, [(i, i ^ 1 << distance) for i in range(lax.axis_siz...  8.97 us
    ppermute x5, waiting for transfers between devices, from_partner(): lax.ppermute(x, axis, [(i, i ^ 1 << distance) for i in range(lax.axis_siz...  8.72 us
    unnamed x26, local copies, waits for them, and re-layouts  7.92 us
    dot_general x1, matrix products, local(): jnp.einsum('lpq,slq->slp', band_blocks[:, 0], leaves, preferred_element_t...  6.93 us
    ppermute x1, starting transfers between devices, extended(): before = lax.ppermute(last, axis, up)  6.22 us
    dot_general x1, matrix products, local(): jnp.einsum('lpq,slq->slp', band_blocks[:, 1], picked, preferred_element_t...  5.92 us
    dot_general x1, matrix products, local(): jnp.einsum('lrp,slp->rls', leaf_basis, leaves, preferred_element_type=jnp...  3.71 us
  transfers between devices with their start and end apart: 7, of which 3 were waited for; matrix products, arithmetic and copies ran while one was open for 24% of the time, Pallas kernels for 0%

commit v1 on v0

v1 whole, which is shorter than its diff:
```python
import functools

import jax
import jax.numpy as jnp
from jax import lax
from jax.experimental import pallas as pl
from jax.experimental.pallas import tpu as pltpu
from jax.sharding import PartitionSpec as P

HW = 16
BF = jnp.bfloat16
F32 = jnp.float32
MESH = pl.DeviceIdType.MESH
PAIR_BASE = (0, 6, 2, 4)
UNROLL = 4


def kernel(
    nx, ny, levels, low_bits,
    offs, pts_h, order_h, lb_h, band_h, tr_h, ob_h, out_h,
    pts, order, xs, ordx, lb, ob, band, tr, tcat, co, snd, rcv, out,
    load_sem, band_sem, out_sem, halo_s, halo_r, lev_s, lev_r,
):
    gx, gy = lax.axis_index("gx"), lax.axis_index("gy")
    me = gx * ny + gy
    last = nx * ny - 1
    rhs = pts.shape[0]
    leaf = xs.shape[1]
    leaves = order.shape[0]
    low_n = xs.shape[0] // rhs
    groups = co.shape[0]
    per = leaves // groups
    rank = co.shape[1]
    width = co.shape[2]
    after0 = HW + leaves

    loads = [
        pltpu.make_async_copy(pts_h, pts, load_sem.at[0]),
        pltpu.make_async_copy(order_h, order, load_sem.at[1]),
        pltpu.make_async_copy(lb_h, lb, load_sem.at[2]),
        pltpu.make_async_copy(tr_h.at[0], tr, load_sem.at[3]),
        pltpu.make_async_copy(ob_h, ob, load_sem.at[4]),
    ]
    quarter = leaves // 4
    band_loads = [
        pltpu.make_async_copy(
            band_h.at[pl.ds(i * quarter, quarter)], band.at[pl.ds(i * quarter, quarter)], band_sem.at[i]
        )
        for i in range(4)
    ]
    for c in loads + band_loads:
        c.start()

    def partner(k):
        if k < low_bits:
            b = 1 << k
            return gx, gy + b - 2 * b * ((gy // b) % 2)
        b = 1 << (k - low_bits)
        return gx + b - 2 * b * ((gx // b) % 2), gy

    low_id = ((me + last) % (last + 1) // ny, (me + last) % (last + 1) % ny)
    high_id = ((me + 1) % (last + 1) // ny, (me + 1) % (last + 1) % ny)
    barrier = pltpu.get_barrier_semaphore()
    for k in range(levels):
        pl.semaphore_signal(barrier, inc=1, device_id=partner(k), device_id_type=MESH)

    @pl.when(me > 0)
    def _():
        pl.semaphore_signal(barrier, inc=1, device_id=low_id, device_id_type=MESH)

    @pl.when(me < last)
    def _():
        pl.semaphore_signal(barrier, inc=1, device_id=high_id, device_id_type=MESH)

    @pl.when(me == 0)
    def _():
        ordx[pl.ds(0, HW)] = jnp.zeros((HW, rhs, leaf), BF)

    @pl.when(me == last)
    def _():
        ordx[pl.ds(after0, HW)] = jnp.zeros((HW, rhs, leaf), BF)

    loads[0].wait()
    for t in range(low_n):
        xs[t * rhs : (t + 1) * rhs, :] = pts[:, t * leaf : (t + 1) * leaf].astype(BF)
    loads[1].wait()

    key_iota = lax.broadcasted_iota(jnp.int32, (leaf, leaf), 0)
    bits = leaf.bit_length() - 1
    lane_leaf = lax.broadcasted_iota(jnp.int32, (rank, width), 1) // rhs

    def gather_leaf(l):
        o = order[pl.ds(l, 1), :]
        onehot = jnp.where(key_iota == (o & (leaf - 1)), 1.0, 0.0).astype(BF)
        high = jnp.broadcast_to(o >> bits, (rhs, leaf))
        full = jnp.dot(xs[...], onehot, preferred_element_type=F32)
        v = [full[t * rhs : (t + 1) * rhs] for t in range(low_n)]
        b = 0
        while len(v) > 1:
            m = ((high >> b) & 1) == 1
            v = [jnp.where(m, v[2 * i + 1], v[2 * i]) for i in range(len(v) // 2)]
            b += 1
        return v[0].astype(BF)

    def gather_pair(q):
        base = PAIR_BASE[q]

        def body(i, _):
            rows = [gather_leaf(base * per + i * UNROLL + u) for u in range(UNROLL)]
            for u in range(UNROLL):
                ordx[HW + base * per + i * UNROLL + u] = rows[u]
            return 0

        lax.fori_loop(0, 2 * per // UNROLL, body, 0)
        if q == 0:
            loads[2].wait()
        for i in range(2):
            g, pos = base + i, 2 * q + i
            f = lax.dot_general(
                lb[g * per * rank : (g + 1) * per * rank, :],
                ordx[HW + g * per : HW + (g + 1) * per].reshape(width, leaf),
                (((1,), (1,)), ((), ())),
                preferred_element_type=F32,
            )
            c = f[:rank]
            for j in range(1, per):
                c = jnp.where(lane_leaf == j, f[j * rank : (j + 1) * rank], c)
            co[pos] = c
            snd[0, pos] = c.astype(BF)

    half = groups // 2

    def level_copy(k, h):
        return pltpu.make_async_remote_copy(
            src_ref=snd.at[k, pl.ds(h * half, half)],
            dst_ref=rcv.at[k, pl.ds(h * half, half)],
            send_sem=lev_s.at[k, h],
            recv_sem=lev_r.at[k, h],
            device_id=partner(k),
            device_id_type=MESH,
        )

    def translate(k, h):
        level_copy(k, h).wait_recv()
        for p in range(half):
            pos = h * half + p
            g = PAIR_BASE[pos // 2] + pos % 2
            c = co[pos]
            ch = c.astype(BF)
            cl = (c - ch.astype(F32)).astype(BF)
            other = rcv[k, pos]
            stacked = jnp.concatenate([ch, cl, ch, other, other], axis=0)
            new = jnp.dot(tcat[k, g], stacked, preferred_element_type=F32)
            co[pos] = new
            if k + 1 < levels:
                snd[k + 1, pos] = new.astype(BF)
        if k + 1 < levels:
            level_copy(k + 1, h).start()

    down = pltpu.make_async_remote_copy(
        src_ref=ordx.at[pl.ds(HW, HW)],
        dst_ref=ordx.at[pl.ds(after0, HW)],
        send_sem=halo_s.at[0],
        recv_sem=halo_r.at[0],
        device_id=low_id,
        device_id_type=MESH,
    )
    up = pltpu.make_async_remote_copy(
        src_ref=ordx.at[pl.ds(after0 - HW, HW)],
        dst_ref=ordx.at[pl.ds(0, HW)],
        send_sem=halo_s.at[1],
        recv_sem=halo_r.at[1],
        device_id=high_id,
        device_id_type=MESH,
    )

    gather_pair(0)
    has_low, has_high = (me + last - 1) // last, (2 * last - me - 1) // last
    pl.semaphore_wait(barrier, levels + has_low + has_high)

    @pl.when(me > 0)
    def _():
        down.start()

    gather_pair(1)
    level_copy(0, 0).start()

    @pl.when(me < last)
    def _():
        up.start()

    loads[3].wait()

    def cat_body(i, _):
        k, g = i // groups, i % groups
        t0, t1 = tr[k, g, 0], tr[k, g, 1]
        h0, h1 = t0.astype(BF).astype(F32), t1.astype(BF).astype(F32)
        tcat[k, g] = jnp.concatenate([h0, h0, t0 - h0, h1, t1 - h1], axis=1).astype(BF)
        return 0

    lax.fori_loop(0, levels * groups, cat_body, 0)
    gather_pair(2)
    translate(0, 0)
    gather_pair(3)
    level_copy(0, 1).start()
    translate(1, 0)

    @pl.when(me < last)
    def _():
        down.wait_recv()

    @pl.when(me > 0)
    def _():
        up.wait_recv()

    def near(seg):
        band_loads[seg].wait()

        def body(i, _):
            l = seg * quarter + i
            own = ordx[l + HW]
            part = ordx[l + HW + offs[l]]
            dims = (((1,), (1,)), ((), ()))
            r = lax.dot_general(own, band[l, 0], dims, preferred_element_type=F32)
            r += lax.dot_general(part, band[l, 1], dims, preferred_element_type=F32)
            out[:, pl.ds(pl.multiple_of(l * leaf, leaf), leaf)] = r
            return 0

        lax.fori_loop(0, quarter, body, 0)

    row_leaf = lax.broadcasted_iota(jnp.int32, (per * rank, width), 0) // rank
    col_leaf = lax.broadcasted_iota(jnp.int32, (per * rank, width), 1) // rhs
    diagonal = row_leaf == col_leaf
    span = per * leaf

    def out_copy(g):
        return pltpu.make_async_copy(
            out.at[:, pl.ds(g * span, span)], out_h.at[:, pl.ds(g * span, span)], out_sem.at[g]
        )

    def far(h):
        for p in range(half):
            pos = h * half + p
            g = PAIR_BASE[pos // 2] + pos % 2
            c = co[pos].astype(BF).astype(F32)
            tiled = jnp.where(diagonal, jnp.concatenate([c] * per, axis=0), 0.0)
            f = lax.dot_general(
                tiled.T.astype(BF),
                ob[g * per * rank : (g + 1) * per * rank, :],
                (((1,), (0,)), ((), ())),
                preferred_element_type=F32,
            )
            for j in range(per):
                at = (g * per + j) * leaf
                out[:, at : at + leaf] = out[:, at : at + leaf] + f[j * rhs : (j + 1) * rhs]
            out_copy(g).start()

    todo = [list(range(2, levels)), list(range(levels))]
    for seg in range(4):
        near(seg)
        for h in range(2):
            if todo[h]:
                translate(todo[h].pop(0), h)
    loads[4].wait()
    while todo[0]:
        for h in range(2):
            if todo[h]:
                translate(todo[h].pop(0), h)
    far(0)
    while todo[1]:
        translate(todo[1].pop(0), 1)
    far(1)

    for k in range(levels):
        for h in range(2):
            level_copy(k, h).wait_send()

    @pl.when(me > 0)
    def _():
        down.wait_send()

    @pl.when(me < last)
    def _():
        up.wait_send()

    for g in range(groups):
        out_copy(g).wait()


def solution(mesh):
    nx, ny = mesh.shape["gx"], mesh.shape["gy"]
    low_bits = ny.bit_length() - 1

    def local(points_rhs, morton_order, band_offsets, leaf_basis, band_blocks, translations, out_basis):
        rhs, points = points_rhs.shape
        leaves, rank, leaf = leaf_basis.shape
        levels, groups = translations.shape[1:3]
        width = leaves // groups * rhs
        anywhere = pl.BlockSpec(memory_space=pl.ANY)
        dma = pltpu.SemaphoreType.DMA
        return pl.pallas_call(
            functools.partial(kernel, nx, ny, levels, low_bits),
            out_shape=jax.ShapeDtypeStruct((rhs, points), F32),
            in_specs=[pl.BlockSpec(memory_space=pltpu.SMEM)] + [anywhere] * 6,
            out_specs=anywhere,
            scratch_shapes=[
                pltpu.VMEM((rhs, points), F32),
                pltpu.VMEM((leaves, leaf), jnp.int32),
                pltpu.VMEM((points // leaf * rhs, leaf), BF),
                pltpu.VMEM((leaves + 2 * HW, rhs, leaf), BF),
                pltpu.VMEM((leaves * rank, leaf), BF),
                pltpu.VMEM((leaves * rank, leaf), BF),
                pltpu.VMEM((leaves, 2, leaf, leaf), BF),
                pltpu.VMEM((levels, groups, 2, rank, rank), F32),
                pltpu.VMEM((levels, groups, rank, 5 * rank), BF),
                pltpu.VMEM((groups, rank, width), F32),
                pltpu.VMEM((levels, groups, rank, width), BF),
                pltpu.VMEM((levels, groups, rank, width), BF),
                pltpu.VMEM((rhs, points), F32),
                dma((5,)),
                dma((4,)),
                dma((groups,)),
                dma((2,)),
                dma((2,)),
                dma((levels, 2)),
                dma((levels, 2)),
            ],
            compiler_params=pltpu.CompilerParams(
                collective_id=0, has_side_effects=True, vmem_limit_bytes=48 * 1024 * 1024
            ),
            cost_estimate=pl.CostEstimate(flops=10**10, bytes_accessed=22 * 10**6, transcendentals=0),
        )(
            band_offsets,
            points_rhs,
            morton_order.reshape(leaves, leaf),
            leaf_basis.reshape(leaves * rank, leaf),
            band_blocks,
            translations,
            out_basis.reshape(leaves * rank, leaf),
        )

    return jax.shard_map(
        local,
        mesh=mesh,
        in_specs=(
            P(None, ("gx", "gy")),
            P(("gx", "gy")),
            P(("gx", "gy")),
            P(("gx", "gy"), None, None),
            P(("gx", "gy"), None, None, None),
            P(("gx", "gy"), None, None, None, None, None),
            P(("gx", "gy"), None, None),
        ),
        out_specs=P(None, ("gx", "gy")),
        check_vma=False,
    )
```

time: 126 us -> 47.1 us (0.37)
  local copies, waits for them, and re-layouts: 77 us -> 7.47 us
  Pallas kernels: 0 us -> 39.3 us
  matrix products: 22.5 us -> 0 us
  starting transfers between devices: 16.5 us -> 0 us
  waiting for transfers between devices: 8.73 us -> 0 us
    gather x2 -> x0, local copies, waits for them, and re-layouts: 59.1 us -> none  [the longest x1 57.7 us: local(): ordered = points_rhs[:, morton_order].astype(jnp.bfloat16)]
    pallas_call x0 -> x1, Pallas kernels: none -> 39.3 us  [local(): pl.pallas_call(functools.partial(kernel, nx, ny, levels, low_bits), out_s...]
    dot_general x14 -> x0, matrix products: 22.5 us -> none  [the longest x1 6.93 us: local(): jnp.einsum('lpq,slq->slp', band_blocks[:, 0], leaves, preferred_element_t...]
    ppermute x7 -> x0, starting transfers between devices: 16.5 us -> none  [the longest x5 8.97 us: from_partner(): lax.ppermute(x, axis, [(i, i ^ 1 << distance) for i in range(lax.axis_siz...]
    ppermute x7 -> x0, waiting for transfers between devices: 8.73 us -> none  [the longest x5 8.72 us: from_partner(): lax.ppermute(x, axis, [(i, i ^ 1 << distance) for i in range(lax.axis_siz...]
    slice x4 -> x0, local copies, waits for them, and re-layouts: 4.47 us -> none  [the longest x2 2.65 us: extended(): last = lax.slice_in_dim(x, length - width, length, axis=dim)]
    convert_element_type x2 -> x0, local copies, waits for them, and re-layouts: 3.64 us -> none  [the longest x1 3.46 us: local(): ordered = points_rhs[:, morton_order].astype(jnp.bfloat16)]
    unnamed x26 -> x11, local copies, waits for them, and re-layouts: 7.92 us -> 6.61 us
  transfers between devices with their start and end apart: 7 -> 0, of which waited for: 3 -> 0; matrix products, arithmetic and copies ran while one was open for 24% -> 0% of each run, Pallas kernels for 0% -> 0%
where the time goes in v1:
time: 47.1 us; the launch traced here: 46.8 us
  Pallas kernels  39.3 us (83%)
  local copies, waits for them, and re-layouts  7.47 us (16%)
    pallas_call x1, Pallas kernels, local(): pl.pallas_call(functools.partial(kernel, nx, ny, levels, low_bits), out_s...  39.3 us
    unnamed x11, local copies, waits for them, and re-layouts  6.61 us

profile of v1, /device:TPU:0, one launch (start us, length us, event | category | flops | bytes accessed | tf_op | source)
XLA Modules:
  0.0 46.8 jit_solution(11749916644562396615)
XLA Ops:
  0.0 0.9 %reshape.9.order_h = s32[64,256]{1,0:T(8,128)S(1)} reshape(s32[16384]{0:T(1024)} %param.8) | data formatting | bytes 131072 | tf_op jit(solution)/shard_map/reshape | solution.py:335
  0.9 0.0 copy-start
  0.9 1.3 %copy-done = f32[1,5,8,2,32,32]{5,4,3,2,1,0:T(8,128)S(1)} copy-done((f32[1,5,8,2,32,32]{5,4,3,2,1,0:T(8,128)S(1)}, f32[1,5,8,2,32,32]{5,4,3,2,1,0:T(8,128)}, u32[]{:S(2)}) %copy-start) | copy-done | bytes 327704
  2.2 0.0 copy-start.1
  2.2 1.2 %copy-done.1 = f32[16,16384]{1,0:T(8,128)S(1)} copy-done((f32[16,16384]{1,0:T(8,128)S(1)}, f32[16,16384]{1,0:T(8,128)}, u32[]{:S(2)}) %copy-start.1) | copy-done | bytes 1048600
  3.4 0.0 copy-start.2
  3.4 1.2 %copy-done.2 = bf16[64,32,256]{2,1,0:T(8,128)(2,1)S(1)} copy-done((bf16[64,32,256]{2,1,0:T(8,128)(2,1)S(1)}, bf16[64,32,256]{2,1,0:T(8,128)(2,1)}, u32[]{:S(2)}) %copy-start.2) | copy-done | bytes 1048600
  4.6 0.0 copy-start.3
  4.6 1.2 %copy-done.3 = bf16[64,32,256]{2,1,0:T(8,128)(2,1)S(1)} copy-done((bf16[64,32,256]{2,1,0:T(8,128)(2,1)S(1)}, bf16[64,32,256]{2,1,0:T(8,128)(2,1)}, u32[]{:S(2)}) %copy-start.3) | copy-done | bytes 1048600
  5.9 0.0 copy-start.4
  5.9 0.7 %copy-done.4 = s32[64]{0:T(128)S(1)} copy-done((s32[64]{0:T(128)S(1)}, s32[64]{0:T(128)}, u32[]{:S(2)}) %copy-start.4) | copy-done | bytes 280
  6.5 39.3 %shard_map.73 = f32[16,16384]{1,0:T(8,128)S(1)} custom-call(s32[64]{0:T(128)S(1)} %copy-done.4, f32[16,16384]{1,0:T(8,128)S(1)} %copy-done.1, s32[64,256]{1,0:T(8,128)S(1)} %reshape.9.order_h, bf16[2048,256]{1,0:T(8,128)(2,1)S(1)} %bitcast.2, bf16[64,2,256,256]{3,2,1,0:T(8,128)(2,1)} %band_h.1, f32[1,5,8,2,32,32]{5,4,3,2,1,0:T(8,128)S(1)} %copy-done, ...), custom_call_target="tpu_custom_call" | custom-call | flops 10000000000 | bytes 22000000 | tf_op jit(solution)/shard_map/pallas_call | solution.py:301
  45.9 1.0 %copy.9 = f32[16,16384]{1,0:T(8,128)} copy(f32[16,16384]{1,0:T(8,128)S(1)} %shard_map.73) | data formatting | bytes 2097152
Async XLA Ops:
  0.9 1.3 %copy-start = (f32[1,5,8,2,32,32]{5,4,3,2,1,0:T(8,128)S(1)}, f32[1,5,8,2,32,32]{5,4,3,2,1,0:T(8,128)}, u32[]{:S(2)}) copy-start(f32[1,5,8,2,32,32]{5,4,3,2,1,0:T(8,128)} %tr_h.1) | copy-start | bytes 983044
  2.2 1.2 %copy-start.1 = (f32[16,16384]{1,0:T(8,128)S(1)}, f32[16,16384]{1,0:T(8,128)}, u32[]{:S(2)}) copy-start(f32[16,16384]{1,0:T(8,128)} %pts_h.1) | copy-start | bytes 3145732
  3.4 1.2 %copy-start.2 = (bf16[64,32,256]{2,1,0:T(8,128)(2,1)S(1)}, bf16[64,32,256]{2,1,0:T(8,128)(2,1)}, u32[]{:S(2)}) copy-start(bf16[64,32,256]{2,1,0:T(8,128)(2,1)} %param.10) | copy-start | bytes 3145732
  4.6 1.2 %copy-start.3 = (bf16[64,32,256]{2,1,0:T(8,128)(2,1)S(1)}, bf16[64,32,256]{2,1,0:T(8,128)(2,1)}, u32[]{:S(2)}) copy-start(bf16[64,32,256]{2,1,0:T(8,128)(2,1)} %param.13) | copy-start | bytes 3145732
  5.9 0.7 %copy-start.4 = (s32[64]{0:T(128)S(1)}, s32[64]{0:T(128)}, u32[]{:S(2)}) copy-start(s32[64]{0:T(128)} %offs.1) | copy-start | bytes 772

commit v2 on v1

--- a/solution.py
+++ b/solution.py
@@ -8,11 +8,13 @@
 from jax.sharding import PartitionSpec as P
 
 HW = 16
+LANES = 128
 BF = jnp.bfloat16
 F32 = jnp.float32
 MESH = pl.DeviceIdType.MESH
 PAIR_BASE = (0, 6, 2, 4)
-UNROLL = 4
+UNROLL = 8
+NEAR_BATCH = 1
 
 
 def kernel(
@@ -26,7 +28,7 @@
     last = nx * ny - 1
     rhs = pts.shape[0]
     leaf = xs.shape[1]
-    leaves = order.shape[0]
+    leaves = band.shape[0]
     low_n = xs.shape[0] // rhs
     groups = co.shape[0]
     per = leaves // groups
@@ -90,7 +92,8 @@
     lane_leaf = lax.broadcasted_iota(jnp.int32, (rank, width), 1) // rhs
 
     def gather_leaf(l):
-        o = order[pl.ds(l, 1), :]
+        parts = order.shape[1]
+        o = jnp.concatenate([order[pl.ds(l * (leaf // parts) + i, 1), :] for i in range(leaf // parts)], axis=1)
         onehot = jnp.where(key_iota == (o & (leaf - 1)), 1.0, 0.0).astype(BF)
         high = jnp.broadcast_to(o >> bits, (rhs, leaf))
         full = jnp.dot(xs[...], onehot, preferred_element_type=F32)
@@ -191,14 +194,14 @@
 
     loads[3].wait()
 
-    def cat_body(i, _):
-        k, g = i // groups, i % groups
-        t0, t1 = tr[k, g, 0], tr[k, g, 1]
-        h0, h1 = t0.astype(BF).astype(F32), t1.astype(BF).astype(F32)
-        tcat[k, g] = jnp.concatenate([h0, h0, t0 - h0, h1, t1 - h1], axis=1).astype(BF)
+    def cat_body(k, _):
+        for g in range(groups):
+            t0, t1 = tr[k, g, 0], tr[k, g, 1]
+            h0, h1 = t0.astype(BF).astype(F32), t1.astype(BF).astype(F32)
+            tcat[k, g] = jnp.concatenate([h0, h0, t0 - h0, h1, t1 - h1], axis=1).astype(BF)
         return 0
 
-    lax.fori_loop(0, levels * groups, cat_body, 0)
+    lax.fori_loop(0, levels, cat_body, 0)
     gather_pair(2)
     translate(0, 0)
     gather_pair(3)
@@ -213,20 +216,29 @@
     def _():
         up.wait_recv()
 
+    leaf_lane = lax.broadcasted_iota(jnp.int32, (leaf, width), 1) // rhs
+
     def near(seg):
         band_loads[seg].wait()
 
-        def body(i, _):
-            l = seg * quarter + i
-            own = ordx[l + HW]
-            part = ordx[l + HW + offs[l]]
+        for g in range(seg * groups // 4, (seg + 1) * groups // 4):
+            own = ordx[HW + g * per : HW + (g + 1) * per].reshape(width, leaf)
+            picked = [ordx[l + HW + offs[l]] for l in range(g * per, (g + 1) * per)]
+            part = jnp.concatenate(picked, axis=0)
             dims = (((1,), (1,)), ((), ()))
-            r = lax.dot_general(own, band[l, 0], dims, preferred_element_type=F32)
-            r += lax.dot_general(part, band[l, 1], dims, preferred_element_type=F32)
-            out[:, pl.ds(pl.multiple_of(l * leaf, leaf), leaf)] = r
-            return 0
-
-        lax.fori_loop(0, quarter, body, 0)
+            total = None
+            for j in range(0, per, NEAR_BATCH):
+                at = pl.ds(g * per + j, NEAR_BATCH)
+                flat = (NEAR_BATCH * leaf, leaf)
+                f = lax.dot_general(band[at, 0].reshape(flat), own, dims, preferred_element_type=F32)
+                f += lax.dot_general(band[at, 1].reshape(flat), part, dims, preferred_element_type=F32)
+                for i in range(NEAR_BATCH):
+                    piece = f[i * leaf : (i + 1) * leaf]
+                    total = piece if total is None else jnp.where(leaf_lane == j + i, piece, total)
+            total = total.T
+            for j in range(per):
+                at = (g * per + j) * leaf
+                out[:, at : at + leaf] = total[j * rhs : (j + 1) * rhs]
 
     row_leaf = lax.broadcasted_iota(jnp.int32, (per * rank, width), 0) // rank
     col_leaf = lax.broadcasted_iota(jnp.int32, (per * rank, width), 1) // rhs
@@ -305,7 +317,7 @@
             out_specs=anywhere,
             scratch_shapes=[
                 pltpu.VMEM((rhs, points), F32),
-                pltpu.VMEM((leaves, leaf), jnp.int32),
+                pltpu.VMEM((points // LANES, LANES), jnp.int32),
                 pltpu.VMEM((points // leaf * rhs, leaf), BF),
                 pltpu.VMEM((leaves + 2 * HW, rhs, leaf), BF),
                 pltpu.VMEM((leaves * rank, leaf), BF),
@@ -326,13 +338,13 @@
                 dma((levels, 2)),
             ],
             compiler_params=pltpu.CompilerParams(
-                collective_id=0, has_side_effects=True, vmem_limit_bytes=48 * 1024 * 1024
+                collective_id=0, has_side_effects=True, vmem_limit_bytes=60 * 1024 * 1024
             ),
             cost_estimate=pl.CostEstimate(flops=10**10, bytes_accessed=22 * 10**6, transcendentals=0),
         )(
             band_offsets,
             points_rhs,
-            morton_order.reshape(leaves, leaf),
+            morton_order.reshape(points // LANES, LANES),
             leaf_basis.reshape(leaves * rank, leaf),
             band_blocks,
             translations,

time: 47.1 us -> 36.6 us (0.78)
  local copies, waits for them, and re-layouts: 7.47 us -> 2.26 us
  Pallas kernels: 39.3 us -> 34.2 us
    pallas_call x1, Pallas kernels: 39.3 us -> 34.2 us  [local(): pl.pallas_call(functools.partial(kernel, nx, ny, levels, low_bits), out_s...]
    unnamed x11 -> x1, local copies, waits for them, and re-layouts: 6.61 us -> 2.26 us
    reshape x1 -> x0, local copies, waits for them, and re-layouts: 0.86 us -> none  [local(): morton_order.reshape(leaves, leaf)]
where the time goes in v2:
time: 36.6 us; the launch traced here: 36.5 us
  Pallas kernels  34.2 us (93%)
  local copies, waits for them, and re-layouts  2.26 us (6%)
    pallas_call x1, Pallas kernels, local(): pl.pallas_call(functools.partial(kernel, nx, ny, levels, low_bits), out_s...  34.2 us
    unnamed x1, local copies, waits for them, and re-layouts  2.26 us

profile of v2, /device:TPU:0, one launch (start us, length us, event | category | flops | bytes accessed | tf_op | source)
XLA Modules:
  0.0 36.5 jit_solution(13715017149130716911)
XLA Ops:
  0.0 34.2 %shard_map.73 = f32[16,16384]{1,0:T(8,128)} custom-call(s32[64]{0:T(128)} %offs.1, f32[16,16384]{1,0:T(8,128)} %pts_h.1, s32[128,128]{1,0:T(8,128)} %bitcast.5, bf16[2048,256]{1,0:T(8,128)(2,1)} %bitcast.3, bf16[64,2,256,256]{3,2,1,0:T(8,128)(2,1)} %band_h.1, f32[1,5,8,2,32,32]{5,4,3,2,1,0:T(8,128)} %tr_h.1, bf16[2048,256]{1,0:T(8,128)(2,1)} %bitcast.4), custom_call_target="tpu_custom_call" | custom-call | flops 10000000000 | bytes 22000000 | tf_op jit(solution)/shard_map/pallas_call | solution.py:313
  34.2 2.3 %copy.9 = f32[16,16384]{1,0:T(8,128)} copy(f32[16,16384]{1,0:T(8,128)} %shard_map.73) | data formatting | bytes 2097152
